TPU v7x, 256 devices: a whole 4x4x8 slice. The times are simulated.
256 devices in a mesh: slot: 16 (over z, core), hid: 16 (over y, x).
Axes of the slice: x: 4, y: 4, z: 8, core: 2. Of those that a mesh axis runs over, the one named last changes fastest.
Arguments:
- cotangent: bfloat16 [32768, 2048], P('slot', 'hid'), may hold values from -6 to 6
- hidden: bfloat16 [32768, 8192], P('slot', 'hid'), may hold values from -6 to 6
- weights: bfloat16 [16, 8192, 2048], P('slot', 'hid'), may hold values from -0.125 to 0.125
- slot_experts: int32 [16, 1], replicated, may hold values from 0 to 3
- next_experts: int32 [16, 1], replicated, may hold values from 0 to 3
- row_counts: int32 [16], replicated, may hold values from 1 to 2048, 20480 in all
- master: float32 [4, 8192, 2048], P(None, 'hid', 'slot'), may hold values from -3 to 3
- momentum: float32 [4, 8192, 2048], P(None, 'hid', 'slot'), may hold values from -96 to 96
Outputs:
- input_grad: bfloat16 [32768, 8192], P('slot', 'hid')
- new_momentum: float32 [4, 8192, 2048], P(None, 'hid', 'slot')
- new_master: float32 [4, 8192, 2048], P(None, 'hid', 'slot')
- placed: bfloat16 [16, 8192, 2048], P('slot', 'hid')
Inputs may be any that keep to these rules, and one draw needn't show every extreme that they name: `slot_experts`: every expert 0 to 3 is held by at least one slot. `next_experts`: every expert 0 to 3 is held by at least one slot. `row_counts`: the counts sum to 20480.
All inputs are finite; a program needn't handle non-finite values.
Results may differ from a plain program's by a relative error of at most 0.015.
Values may be sent and summed in bfloat16 or wider, within the bound.
No kernel may reach another device: no remote copies, remote signals or barrier semaphores. Data moves between devices by JAX's collectives and lax.ppermute only.
A program may use at most 128 MiB of HBM per device.

v0:
```python
import jax
import jax.numpy as jnp
from jax import lax
from jax.sharding import PartitionSpec as P

momentum_decay = 0.9
learn_rate = 0.01


def local(cotangent, hidden, weights, slot_experts, next_experts, row_counts, master, momentum):
    row_span = hidden.shape[0]
    own_slot = lax.axis_index("slot")
    live_count = lax.dynamic_index_in_dim(row_counts, own_slot, 0, keepdims=False)
    live_mask = (jnp.arange(row_span, dtype=jnp.int32) < live_count)[:, None].astype(
        cotangent.dtype
    )
    masked = cotangent * live_mask
    weight_rows = weights[0]
    shard_piece = lax.all_gather(masked, "hid", axis=1, tiled=True)
    hid_grad = lax.dot_general(
        shard_piece, weight_rows, (((1,), (1,)), ((), ())), preferred_element_type=jnp.float32
    )
    w_part = lax.dot_general(
        hidden, shard_piece, (((0,), (0,)), ((), ())), preferred_element_type=jnp.float32
    )
    w_grad = w_part
    hid_grad, w_grad = (hid_grad, w_grad)
    input_grad = hid_grad.astype(jnp.bfloat16)
    expert_count = master.shape[0]
    owners = (
        slot_experts[:, 0][None, :] == jnp.arange(expert_count, dtype=jnp.int32)[:, None]
    ).astype(jnp.float32)
    own_weight = lax.dynamic_index_in_dim(owners, own_slot, 1, keepdims=False)
    stacked = own_weight[:, None, None] * w_grad[None]
    expert_grad = lax.psum_scatter(
        stacked.astype(jnp.bfloat16), "slot", scatter_dimension=2, tiled=True
    ).astype(jnp.float32)
    new_momentum = momentum_decay * momentum + expert_grad
    new_master = master - learn_rate * new_momentum
    rounded = new_master.astype(jnp.bfloat16)
    gathered = lax.all_gather(rounded, "slot", axis=2, tiled=True)
    target = lax.dynamic_index_in_dim(next_experts[:, 0], own_slot, 0, keepdims=False)
    placed = lax.dynamic_index_in_dim(gathered, target, 0, keepdims=True)
    return (input_grad, new_momentum, new_master, placed)


def solution(mesh):
    return jax.shard_map(
        local,
        mesh=mesh,
        in_specs=(
            P("slot", "hid"),
            P("slot", "hid"),
            P("slot", "hid", None),
            P(),
            P(),
            P(),
            P(None, "hid", "slot"),
            P(None, "hid", "slot"),
        ),
        out_specs=(
            P("slot", "hid"),
            P(None, "hid", "slot"),
            P(None, "hid", "slot"),
            P("slot", "hid", None),
        ),
        check_vma=False,
    )
```

profile of v0, /device:TPU:1, one launch (start us, length us, event | category | flops | bytes accessed | tf_op | source)
XLA Modules:
  0.0 297.3 jit_solution(14528464055429409936)
XLA Ops:
  7.2 0.0 copy-start
  7.2 0.0 all-gather.3.cloned.1.call-start
  7.2 1.4 dynamic_slice.15
  8.6 0.6 fusion.1
  9.3 2.2 broadcast_multiply_fusion
  11.4 0.0 all-gather.3.cloned.1.call-update
  11.5 0.0 reduce-scatter.4.cloned.1.call-start
  11.5 1.2 dynamic-slice.1
  12.8 0.6 fusion.2
  13.4 84.5 %all-gather.3.cloned.1.call-done = bf16[2048,2048]{1,0:T(8,128)(2,1)} async-done(((bf16[2048,128]{1,0:T(8,128)(2,1)}), bf16[2048,2048]{1,0:T(8,128)(2,1)}) %all-gather.3.cloned.1.call-update) | async-done | bytes 8388624 | tf_op jit(solution)/shard_map/all_gather | solution.py:19
  97.9 0.0 copy-done
  97.9 9.8 %convolution_bitcast_fusion = f32[512,2048]{0,1:T(8,128)} fusion(bf16[2048,2048]{1,0:T(8,128)(2,1)} %all-gather.3.cloned.1.call-done, bf16[2048,512]{1,0:T(8,128)(2,1)S(1)} %copy-done), kind=kOutput, calls=%fused_computation.1 | convolution fusion | flops 4294967296 | bytes 14680064 | tf_op jit(solution)/shard_map/dot_general | solution.py:23
  107.7 5.5 %copy.13 = f32[512,2048]{1,0:T(8,128)} copy(f32[512,2048]{0,1:T(8,128)} %convolution_bitcast_fusion) | data formatting | bytes 8388608 | tf_op jit(solution)/shard_map/dot_general | solution.py:23
  113.1 8.0 %multiply_convert_fusion = bf16[4,512,2048]{2,1,0:T(8,128)(2,1)} fusion(f32[512,2048]{1,0:T(8,128)} %copy.13, f32[4]{0:T(128)S(1)} %fusion.2), kind=kLoop, calls=%fused_computation | loop fusion | flops 8388608 | bytes 12582928 | tf_op jit(solution)/shard_map/convert_element_type | solution.py:36
  121.1 14.6 %copy.14 = bf16[4,512,2048]{1,0,2:T(4,128)(2,1)} copy(bf16[4,512,2048]{2,1,0:T(8,128)(2,1)} %multiply_convert_fusion) | data formatting | bytes 16777216
  135.7 10.2 %copy.16 = bf16[256,8,4,512]{3,1,2,0:T(8,128)(2,1)} copy(bf16[256,8,4,512]{3,2,1,0:T(4,128)(2,1)} %bitcast.18) | data formatting | bytes 16777216
  146.0 0.0 reduce-scatter.4.cloned.1.call-update
  146.0 0.0 copy-start.1
  146.0 0.2 all-gather.5.cloned.1.call-start
  146.2 68.0 %reduce-scatter.4.cloned.1.call-done = bf16[128,2048]{1,0:T(8,128)(2,1)} async-done(((bf16[2048,2048]{1,0:T(8,128)(2,1)}), bf16[128,2048]{1,0:T(8,128)(2,1)}) %reduce-scatter.4.cloned.1.call-update) | async-done | bytes 524304
  214.3 1.4 reshape.21
  215.7 0.4 copy.15
  216.1 3.2 %fusion.3 = (bf16[4,512,128]{2,1,0:T(8,128)(2,1)}, f32[4,512,128]{2,1,0:T(8,128)}, f32[4,512,128]{2,1,0:T(8,128)}) fusion(f32[4,512,128]{2,1,0:T(8,128)} %param.14, bf16[4,512,128]{2,1,0:T(8,128)(2,1)S(1)} %copy.15, f32[4,512,128]{2,1,0:T(8,128)} %param.15), kind=kLoop, calls=%fused_computation.13 | loop fusion | flops 1572864 | bytes 5242880 | tf_op jit(solution)/shard_map/convert_element_type | solution.py:40
  219.4 0.0 all-gather.5.cloned.1.call-update
  219.4 0.0 copy-done.1
  219.4 0.6 constant_dynamic-slice_fusion
  221.9 9.9 %convolution_convert_fusion = bf16[2048,512]{1,0:T(8,128)(2,1)} fusion(bf16[2048,2048]{1,0:T(8,128)(2,1)} %all-gather.3.cloned.1.call-done, bf16[1,512,2048]{2,1,0:T(8,128)(2,1)} %param.10), kind=kOutput, calls=%fused_computation.2 | convolution fusion | flops 4296015872 | bytes 12582912 | tf_op jit(solution)/shard_map/dot_general | solution.py:20
  231.8 55.9 %all-gather.5.cloned.1.call-done = bf16[4,512,2048]{2,1,0:T(8,128)(2,1)} async-done(((bf16[4,512,128]{2,1,0:T(8,128)(2,1)}), bf16[4,512,2048]{2,1,0:T(8,128)(2,1)}) %all-gather.5.cloned.1.call-update) | async-done | bytes 8388624 | tf_op jit(solution)/shard_map/all_gather | solution.py:41
  287.6 3.2 %constant_dynamic-slice_fusion.1 = bf16[1,512,2048]{2,1,0:T(8,128)(2,1)} fusion(bf16[4,512,2048]{2,1,0:T(8,128)(2,1)} %all-gather.5.cloned.1.call-done, s32[]{:T(128)S(6)} %select_n.12), kind=kLoop, calls=%fused_computation.12 | loop fusion | bytes 4194308 | tf_op jit(solution)/shard_map/jit(dynamic_index_in_dim)/dynamic_slice | solution.py:43
Async XLA Ops:
  7.2 90.8 %copy-start = (bf16[2048,512]{1,0:T(8,128)(2,1)S(1)}, bf16[2048,512]{1,0:T(8,128)(2,1)}, u32[]{:S(2)}) copy-start(bf16[2048,512]{1,0:T(8,128)(2,1)} %param.9) | copy-start | bytes 6291460
  7.2 90.7 %all-gather.3.cloned.1.call-start = ((), (), s32[]{:S(2)}) async-start(), calls=%async_computation.1 | async-start | bytes 8912896 | tf_op jit(solution)/shard_map/all_gather | solution.py:19
  11.5 202.8 %reduce-scatter.4.cloned.1.call-start = ((), (), s32[]{:S(2)}) async-start(), calls=%async_computation.3 | async-start | bytes 8912896
  146.0 73.4 %copy-start.1 = (s32[16,1]{0,1:T(1,128)S(1)}, s32[16,1]{0,1:T(1,128)}, u32[]{:S(2)}) copy-start(s32[16,1]{0,1:T(1,128)} %param.12) | copy-start | bytes 196
  146.0 141.6 %all-gather.5.cloned.1.call-start = ((), (), s32[]{:S(2)}) async-start(), calls=%async_computation.2 | async-start | bytes 8912896 | tf_op jit(solution)/shard_map/all_gather | solution.py:41
Sparse Core Ops, SparseCore 0:
  11.6 86.2 all-gather.2
  146.1 68.1 reduce-scatter.3
  219.5 68.0 all-gather.4
where the time goes:
time: 298 us; the launch traced here: 297 us
  waiting for transfers between devices  208 us (70%)
  local copies, waits for them, and re-layouts  38.5 us (13%)
  matrix products  19.6 us (7%)
  between operations  15.7 us (5%)
  other arithmetic  14.7 us (5%)
    all_gather x1, waiting for transfers between devices, local(): shard_piece = lax.all_gather(masked, 'hid', axis=1, tiled=True)  84.5 us
    unnamed x4, waiting for transfers between devices  68.1 us
    all_gather x1, waiting for transfers between devices, local(): gathered = lax.all_gather(rounded, 'slot', axis=2, tiled=True)  55.9 us
    unnamed x8, local copies, waits for them, and re-layouts  26.7 us
    dot_general x1, matrix products, local(): lax.dot_general(shard_piece, weight_rows, (((1,), (1,)), ((), ())), prefe...  9.86 us
    dot_general x1, matrix products, local(): lax.dot_general(hidden, shard_piece, (((0,), (0,)), ((), ())), preferred_...  9.75 us
    convert_element_type x1, other arithmetic, local(): stacked.astype(jnp.bfloat16)  8 us
  transfers between devices with their start and end apart: 3, of which 3 were waited for; matrix products, arithmetic and copies ran while one was open for 4% of the time, Pallas kernels for 0%

commit v1 on v0

--- a/solution.py
+++ b/solution.py
@@ -5,6 +5,28 @@
 
 momentum_decay = 0.9
 learn_rate = 0.01
+
+
+def joined_along(blocks, dim):
+    shape = list(blocks.shape[1:])
+    shape[dim] *= blocks.shape[0]
+    return jnp.moveaxis(blocks, 0, dim).reshape(shape)
+
+
+def collect(shard, axis, dim):
+    length = lax.axis_size(axis)
+    pairs = [(i, (i + 1) % length) for i in range(length)]
+    back = [(b, a) for a, b in pairs]
+    lower, upper = ([], [])
+    for step in range(length - 1):
+        if step % 2 == 0:
+            lower.append(lax.ppermute(lower[-1] if lower else shard, axis, pairs))
+        else:
+            upper.append(lax.ppermute(upper[-1] if upper else shard, axis, back))
+    pieces = jnp.stack([*lower[::-1], shard, *upper])
+    shift = lax.axis_index(axis) - len(lower)
+    pieces = pieces[(jnp.arange(length) - shift) % length]
+    return joined_along(pieces, dim)
 
 
 def local(cotangent, hidden, weights, slot_experts, next_experts, row_counts, master, momentum):
@@ -16,7 +38,7 @@
     )
     masked = cotangent * live_mask
     weight_rows = weights[0]
-    shard_piece = lax.all_gather(masked, "hid", axis=1, tiled=True)
+    shard_piece = collect(masked, "hid", 1)
     hid_grad = lax.dot_general(
         shard_piece, weight_rows, (((1,), (1,)), ((), ())), preferred_element_type=jnp.float32
     )

time: 298 us -> 367 us (1.23)
  local copies, waits for them, and re-layouts: 38.5 us -> 82.6 us
  starting transfers between devices: 0.3 us -> 37.4 us
  waiting for transfers between devices: 208 us -> 196 us
    all_gather x1 -> x0, waiting for transfers between devices: 84.5 us -> none  [local(): shard_piece = lax.all_gather(masked, 'hid', axis=1, tiled=True)]
    ppermute x0 -> x15, waiting for transfers between devices: none -> 63.4 us  [the longest x8 63.1 us: collect(): lower.append(lax.ppermute(lower[-1] if lower else shard, axis, pairs))]
    ppermute x0 -> x15, starting transfers between devices: none -> 37.1 us  [the longest x7 35 us: collect(): upper.append(lax.ppermute(upper[-1] if upper else shard, axis, back))]
    unnamed x8 -> x56, local copies, waits for them, and re-layouts: 26.7 us -> 49.4 us
    transpose x0 -> x1, local copies, waits for them, and re-layouts: none -> 12.4 us  [joined_along(): return jnp.moveaxis(blocks, 0, dim).reshape(shape)]
    unnamed x4 -> x3, waiting for transfers between devices: 68.1 us -> 77.2 us
    gather x0 -> x1, local copies, waits for them, and re-layouts: none -> 8.17 us  [collect(): pieces = pieces[(jnp.arange(length) - shift) % length]]
  transfers between devices with their start and end apart: 3 -> 17, of which waited for: 3 -> 11; matrix products, arithmetic and copies ran while one was open for 4% -> 10% of each run, Pallas kernels for 0% -> 0%
where the time goes in v1:
time: 367 us; the launch traced here: 366 us
  waiting for transfers between devices  196 us (53%)
  local copies, waits for them, and re-layouts  82.6 us (23%)
  starting transfers between devices  37.4 us (10%)
  matrix products  19.5 us (5%)
  between operations  16.2 us (4%)
  other arithmetic  13.6 us (4%)
    unnamed x3, waiting for transfers between devices  77.2 us
    ppermute x8, waiting for transfers between devices, collect(): lower.append(lax.ppermute(lower[-1] if lower else shard, axis, pairs))  63.1 us
    all_gather x1, waiting for transfers between devices, local(): gathered = lax.all_gather(rounded, 'slot', axis=2, tiled=True)  55.9 us
    unnamed x56, local copies, waits for them, and re-layouts  49.4 us
    ppermute x7, starting transfers between devices, collect(): upper.append(lax.ppermute(upper[-1] if upper else shard, axis, back))  35 us
    transpose x1, local copies, waits for them, and re-layouts, joined_along(): return jnp.moveaxis(blocks, 0, dim).reshape(shape)  12.4 us
    dot_general x1, matrix products, local(): lax.dot_general(shard_piece, weight_rows, (((1,), (1,)), ((), ())), prefe...  10 us
    dot_general x1, matrix products, local(): lax.dot_general(hidden, shard_piece, (((0,), (0,)), ((), ())), preferred_...  9.46 us
  transfers between devices with their start and end apart: 17, of which 11 were waited for; matrix products, arithmetic and copies ran while one was open for 10% of the time, Pallas kernels for 0%

profile of v1, /device:TPU:1, one launch (start us, length us, event | category | flops | bytes accessed | tf_op | source)
XLA Modules:
  0.0 365.8 jit_solution(16002875004977719110)
XLA Ops:
  7.2 1.4 dynamic_slice.15
  9.3 1.4 broadcast_multiply_fusion
  10.7 2.1 collective-permute-start
  12.8 13.4 %collective-permute-done = bf16[2048,128]{1,0:T(8,128)(2,1)S(1)} collective-permute-done((bf16[2048,128]{1,0:T(8,128)(2,1)S(1)}, bf16[2048,128]{1,0:T(8,128)(2,1)S(1)}, u32[]{:S(2)}, u32[]{:S(2)}) %collective-permute-start) | collective-permute-done | bytes 524320 | tf_op jit(solution)/shard_map/ppermute | solution.py:23
  26.2 4.8 %collective-permute-start.8 = (bf16[2048,128]{1,0:T(8,128)(2,1)S(1)}, bf16[2048,128]{1,0:T(8,128)(2,1)S(1)}, u32[]{:S(2)}, u32[]{:S(2)}) collective-permute-start(bf16[2048,128]{1,0:T(8,128)(2,1)S(1)} %broadcast_multiply_fusion), channel_id=1, source_target_pairs={{1,0},{2,1},{3,2},{4,3},{5,4},{6,5},{7,6},{8,7},{9,8},{10,9},{11,1... | collective-permute-start | bytes 1572872 | tf_op jit(solution)/shard_map/ppermute | solution.py:25
  31.0 8.8 %collective-permute-done.1 = bf16[2048,128]{1,0:T(8,128)(2,1)S(1)} collective-permute-done((bf16[2048,128]{1,0:T(8,128)(2,1)S(1)}, bf16[2048,128]{1,0:T(8,128)(2,1)S(1)}, u32[]{:S(2)}, u32[]{:S(2)}) %collective-permute-start.1) | collective-permute-done | bytes 524320 | tf_op jit(solution)/shard_map/ppermute | solution.py:23
  40.6 4.7 %collective-permute-start.9 = (bf16[2048,128]{1,0:T(8,128)(2,1)S(1)}, bf16[2048,128]{1,0:T(8,128)(2,1)S(1)}, u32[]{:S(2)}, u32[]{:S(2)}) collective-permute-start(bf16[2048,128]{1,0:T(8,128)(2,1)S(1)} %collective-permute-done.8), channel_id=1, source_target_pairs={{1,0},{2,1},{3,2},{4,3},{5,4},{6,5},{7,6},{8,7},{9,8},{10,9},{11,1... | collective-permute-start | bytes 1572872 | tf_op jit(solution)/shard_map/ppermute | solution.py:25
  45.4 7.1 %collective-permute-done.2 = bf16[2048,128]{1,0:T(8,128)(2,1)S(1)} collective-permute-done((bf16[2048,128]{1,0:T(8,128)(2,1)S(1)}, bf16[2048,128]{1,0:T(8,128)(2,1)S(1)}, u32[]{:S(2)}, u32[]{:S(2)}) %collective-permute-start.2) | collective-permute-done | bytes 524320 | tf_op jit(solution)/shard_map/ppermute | solution.py:23
  52.5 5.3 %collective-permute-start.10 = (bf16[2048,128]{1,0:T(8,128)(2,1)S(1)}, bf16[2048,128]{1,0:T(8,128)(2,1)S(1)}, u32[]{:S(2)}, u32[]{:S(2)}) collective-permute-start(bf16[2048,128]{1,0:T(8,128)(2,1)S(1)} %collective-permute-done.9), channel_id=1, source_target_pairs={{1,0},{2,1},{3,2},{4,3},{5,4},{6,5},{7,6},{8,7},{9,8},{10,9},{11,1... | collective-permute-start | bytes 1572872 | tf_op jit(solution)/shard_map/ppermute | solution.py:25
  57.7 6.4 %collective-permute-done.3 = bf16[2048,128]{1,0:T(8,128)(2,1)S(1)} collective-permute-done((bf16[2048,128]{1,0:T(8,128)(2,1)S(1)}, bf16[2048,128]{1,0:T(8,128)(2,1)S(1)}, u32[]{:S(2)}, u32[]{:S(2)}) %collective-permute-start.3) | collective-permute-done | bytes 524320 | tf_op jit(solution)/shard_map/ppermute | solution.py:23
  64.2 4.9 %collective-permute-start.11 = (bf16[2048,128]{1,0:T(8,128)(2,1)S(1)}, bf16[2048,128]{1,0:T(8,128)(2,1)S(1)}, u32[]{:S(2)}, u32[]{:S(2)}) collective-permute-start(bf16[2048,128]{1,0:T(8,128)(2,1)S(1)} %collective-permute-done.10), channel_id=1, source_target_pairs={{1,0},{2,1},{3,2},{4,3},{5,4},{6,5},{7,6},{8,7},{9,8},{10,9},{11,1... | collective-permute-start | bytes 1572872 | tf_op jit(solution)/shard_map/ppermute | solution.py:25
  69.1 6.4 %collective-permute-done.4 = bf16[2048,128]{1,0:T(8,128)(2,1)S(1)} collective-permute-done((bf16[2048,128]{1,0:T(8,128)(2,1)S(1)}, bf16[2048,128]{1,0:T(8,128)(2,1)S(1)}, u32[]{:S(2)}, u32[]{:S(2)}) %collective-permute-start.4) | collective-permute-done | bytes 524320 | tf_op jit(solution)/shard_map/ppermute | solution.py:23
  76.3 4.9 %collective-permute-start.12 = (bf16[2048,128]{1,0:T(8,128)(2,1)S(1)}, bf16[2048,128]{1,0:T(8,128)(2,1)}, u32[]{:S(2)}, u32[]{:S(2)}) collective-permute-start(bf16[2048,128]{1,0:T(8,128)(2,1)S(1)} %collective-permute-done.11), channel_id=1, source_target_pairs={{1,0},{2,1},{3,2},{4,3},{5,4},{6,5},{7,6},{8,7},{9,8},{10,9},{11,1... | collective-permute-start | bytes 1572872 | tf_op jit(solution)/shard_map/ppermute | solution.py:25
  81.2 6.3 %collective-permute-done.5 = bf16[2048,128]{1,0:T(8,128)(2,1)S(1)} collective-permute-done((bf16[2048,128]{1,0:T(8,128)(2,1)S(1)}, bf16[2048,128]{1,0:T(8,128)(2,1)S(1)}, u32[]{:S(2)}, u32[]{:S(2)}) %collective-permute-start.5) | collective-permute-done | bytes 524320 | tf_op jit(solution)/shard_map/ppermute | solution.py:23
  87.7 5.3 %collective-permute-start.13 = (bf16[2048,128]{1,0:T(8,128)(2,1)}, bf16[2048,128]{1,0:T(8,128)(2,1)}, u32[]{:S(2)}, u32[]{:S(2)}) collective-permute-start(bf16[2048,128]{1,0:T(8,128)(2,1)} %collective-permute-done.12), channel_id=1, source_target_pairs={{1,0},{2,1},{3,2},{4,3},{5,4},{6,5},{7,6},{8,7},{9,8},{10,9},{11,1... | collective-permute-start | bytes 1572872 | tf_op jit(solution)/shard_map/ppermute | solution.py:25
  93.1 7.7 %collective-permute-done.6 = bf16[2048,128]{1,0:T(8,128)(2,1)} collective-permute-done((bf16[2048,128]{1,0:T(8,128)(2,1)S(1)}, bf16[2048,128]{1,0:T(8,128)(2,1)}, u32[]{:S(2)}, u32[]{:S(2)}) %collective-permute-start.6) | collective-permute-done | bytes 524320 | tf_op jit(solution)/shard_map/ppermute | solution.py:23
  100.7 1.2 dynamic-slice.1
  102.7 5.0 %collective-permute-start.14 = (bf16[2048,128]{1,0:T(8,128)(2,1)}, bf16[2048,128]{1,0:T(8,128)(2,1)S(1)}, u32[]{:S(2)}, u32[]{:S(2)}) collective-permute-start(bf16[2048,128]{1,0:T(8,128)(2,1)} %collective-permute-done.13), channel_id=1, source_target_pairs={{1,0},{2,1},{3,2},{4,3},{5,4},{6,5},{7,6},{8,7},{9,8},{10,9},{11,1... | collective-permute-start | bytes 1572872 | tf_op jit(solution)/shard_map/ppermute | solution.py:25
  107.8 7.1 %collective-permute-done.7 = bf16[2048,128]{1,0:T(8,128)(2,1)} collective-permute-done((bf16[2048,128]{1,0:T(8,128)(2,1)}, bf16[2048,128]{1,0:T(8,128)(2,1)}, u32[]{:S(2)}, u32[]{:S(2)}) %collective-permute-start.7) | collective-permute-done | bytes 524320 | tf_op jit(solution)/shard_map/ppermute | solution.py:23
  114.9 1.9 bitcast_dynamic-update-slice_fusion.15
  116.8 1.9 bitcast_dynamic-update-slice_fusion.14
  118.7 1.9 bitcast_dynamic-update-slice_fusion.13
  120.6 1.9 bitcast_dynamic-update-slice_fusion.12
  122.4 1.9 bitcast_dynamic-update-slice_fusion.11
  124.3 1.9 bitcast_dynamic-update-slice_fusion.10
  126.2 1.9 bitcast_dynamic-update-slice_fusion.9
  128.1 0.8 bitcast_dynamic-update-slice_fusion.8
  128.9 1.1 bitcast_dynamic-update-slice_fusion.7
  130.0 0.8 bitcast_dynamic-update-slice_fusion.6
  130.9 0.8 bitcast_dynamic-update-slice_fusion.5
  131.7 0.9 bitcast_dynamic-update-slice_fusion.4
  132.6 0.8 bitcast_dynamic-update-slice_fusion.3
  133.4 1.9 bitcast_dynamic-update-slice_fusion.2
  135.3 1.9 bitcast_dynamic-update-slice_fusion.1
  137.2 0.9 bitcast_dynamic-update-slice_fusion
  138.1 8.2 %gather_fusion = bf16[16,2048,128]{2,1,0:T(8,128)(2,1)} fusion(bf16[16,2048,128]{2,1,0:T(8,128)(2,1)} %bitcast_dynamic-update-slice_fusion, s32[1024]{0:T(1024)S(1)} %pad_clamp_fusion), kind=kCustom, calls=%fused_computation | custom fusion | bytes 16777280 | tf_op jit(solution)/shard_map/gather | solution.py:28
  146.2 12.4 %copy.16 = bf16[2048,16,128]{0,2,1:T(8,128)(2,1)} copy(bf16[2048,16,128]{2,0,1:T(8,128)(2,1)} %bitcast.53) | data formatting | bytes 16777216 | tf_op jit(solution)/shard_map/transpose | solution.py:13
  158.6 9.5 %convolution_bitcast_fusion = f32[512,2048]{0,1:T(8,128)} fusion(bf16[2048,2048]{0,1:T(8,128)(2,1)} %bitcast.56, bf16[2048,512]{1,0:T(8,128)(2,1)S(1)} %copy-done), kind=kOutput, calls=%fused_computation.2 | convolution fusion | flops 4294967296 | bytes 14680064 | tf_op jit(solution)/shard_map/dot_general | solution.py:45
  168.1 5.4 %copy.17 = f32[512,2048]{1,0:T(8,128)} copy(f32[512,2048]{0,1:T(8,128)} %convolution_bitcast_fusion) | data formatting | bytes 8388608 | tf_op jit(solution)/shard_map/dot_general | solution.py:45
  173.4 8.0 %multiply_convert_fusion = bf16[4,512,2048]{2,1,0:T(8,128)(2,1)} fusion(f32[512,2048]{1,0:T(8,128)} %copy.17, f32[4]{0:T(128)S(1)} %fusion.2), kind=kLoop, calls=%fused_computation.1 | loop fusion | flops 8388608 | bytes 12582928 | tf_op jit(solution)/shard_map/convert_element_type | solution.py:58
  181.5 14.5 %copy.18 = bf16[4,512,2048]{1,0,2:T(4,128)(2,1)} copy(bf16[4,512,2048]{2,1,0:T(8,128)(2,1)} %multiply_convert_fusion) | data formatting | bytes 16777216
  196.0 10.3 %copy.20 = bf16[256,8,4,512]{3,1,2,0:T(8,128)(2,1)} copy(bf16[256,8,4,512]{3,2,1,0:T(4,128)(2,1)} %bitcast.55) | data formatting | bytes 16777216
  206.6 77.1 %reduce-scatter.4.cloned.1.call-done = bf16[128,2048]{1,0:T(8,128)(2,1)} async-done(((bf16[2048,2048]{1,0:T(8,128)(2,1)}), bf16[128,2048]{1,0:T(8,128)(2,1)}) %reduce-scatter.4.cloned.1.call-update) | async-done | bytes 524304
  283.7 1.4 reshape.82
  285.6 1.7 fusion.5
  289.8 10.0 %convolution_convert_fusion = bf16[2048,512]{1,0:T(8,128)(2,1)} fusion(bf16[2048,2048]{0,1:T(8,128)(2,1)} %bitcast.57, bf16[1,512,2048]{2,1,0:T(8,128)(2,1)} %param.10), kind=kOutput, calls=%fused_computation.3 | convolution fusion | flops 4296015872 | bytes 12582912 | tf_op jit(solution)/shard_map/dot_general | solution.py:42
  299.9 55.9 %all-gather.2.cloned.1.call-done = bf16[4,512,2048]{2,1,0:T(8,128)(2,1)} async-done(((bf16[4,512,128]{2,1,0:T(8,128)(2,1)}), bf16[4,512,2048]{2,1,0:T(8,128)(2,1)}) %all-gather.2.cloned.1.call-update) | async-done | bytes 8388624 | tf_op jit(solution)/shard_map/all_gather | solution.py:63
  355.8 3.2 constant_dynamic-slice_fusion.1
  (62 shorter events, 4.7 us)
Async XLA Ops:
  7.2 151.4 %copy-start = (bf16[2048,512]{1,0:T(8,128)(2,1)S(1)}, bf16[2048,512]{1,0:T(8,128)(2,1)}, u32[]{:S(2)}) copy-start(bf16[2048,512]{1,0:T(8,128)(2,1)} %param.9) | copy-start | bytes 6291460
  7.2 121.7 %copy-start.2 = (bf16[2048,128]{1,0:T(8,128)(2,1)S(1)}, bf16[2048,128]{1,0:T(8,128)(2,1)}, u32[]{:S(2)}) copy-start(bf16[2048,128]{1,0:T(8,128)(2,1)} %param.8) | copy-start | bytes 1572868
  7.2 276.5 %reduce-scatter.4.cloned.1.call-start = ((), (), s32[]{:S(2)}) async-start(), calls=%async_computation.2 | async-start | bytes 8912896
  10.7 15.5 %collective-permute-start = (bf16[2048,128]{1,0:T(8,128)(2,1)S(1)}, bf16[2048,128]{1,0:T(8,128)(2,1)S(1)}, u32[]{:S(2)}, u32[]{:S(2)}) collective-permute-start(bf16[2048,128]{1,0:T(8,128)(2,1)S(1)} %broadcast_multiply_fusion), channel_id=1, source_target_pairs={{0,1},{1,2},{2,3},{3,4},{4,5},{5,6},{6,7},{7,8},{8,9},{9,10},{10,1... | collective-permute-start | bytes 1572872 | tf_op jit(solution)/shard_map/ppermute | solution.py:23
  26.2 13.6 %collective-permute-start.1 = (bf16[2048,128]{1,0:T(8,128)(2,1)S(1)}, bf16[2048,128]{1,0:T(8,128)(2,1)S(1)}, u32[]{:S(2)}, u32[]{:S(2)}) collective-permute-start(bf16[2048,128]{1,0:T(8,128)(2,1)S(1)} %collective-permute-done), channel_id=1, source_target_pairs={{0,1},{1,2},{2,3},{3,4},{4,5},{5,6},{6,7},{7,8},{8,9},{9,10},{10,1... | collective-permute-start | bytes 1572872 | tf_op jit(solution)/shard_map/ppermute | solution.py:23
  26.2 13.6 %collective-permute-start.8 = (bf16[2048,128]{1,0:T(8,128)(2,1)S(1)}, bf16[2048,128]{1,0:T(8,128)(2,1)S(1)}, u32[]{:S(2)}, u32[]{:S(2)}) collective-permute-start(bf16[2048,128]{1,0:T(8,128)(2,1)S(1)} %broadcast_multiply_fusion), channel_id=1, source_target_pairs={{1,0},{2,1},{3,2},{4,3},{5,4},{6,5},{7,6},{8,7},{9,8},{10,9},{11,1... | collective-permute-start | bytes 1572872 | tf_op jit(solution)/shard_map/ppermute | solution.py:25
  39.8 12.6 %copy-start.7 = (bf16[2048,128]{1,0:T(8,128)(2,1)}, bf16[2048,128]{1,0:T(8,128)(2,1)S(1)}, u32[]{:S(2)}) copy-start(bf16[2048,128]{1,0:T(8,128)(2,1)S(1)} %collective-permute-done.1) | copy-start | bytes 1572868
  39.8 12.6 %collective-permute-start.2 = (bf16[2048,128]{1,0:T(8,128)(2,1)S(1)}, bf16[2048,128]{1,0:T(8,128)(2,1)S(1)}, u32[]{:S(2)}, u32[]{:S(2)}) collective-permute-start(bf16[2048,128]{1,0:T(8,128)(2,1)S(1)} %collective-permute-done.1), channel_id=1, source_target_pairs={{0,1},{1,2},{2,3},{3,4},{4,5},{5,6},{6,7},{7,8},{8,9},{9,10},{10,1... | collective-permute-start | bytes 1572872 | tf_op jit(solution)/shard_map/ppermute | solution.py:23
  39.8 0.8 copy-start.5
  40.6 11.8 %collective-permute-start.9 = (bf16[2048,128]{1,0:T(8,128)(2,1)S(1)}, bf16[2048,128]{1,0:T(8,128)(2,1)S(1)}, u32[]{:S(2)}, u32[]{:S(2)}) collective-permute-start(bf16[2048,128]{1,0:T(8,128)(2,1)S(1)} %collective-permute-done.8), channel_id=1, source_target_pairs={{1,0},{2,1},{3,2},{4,3},{5,4},{6,5},{7,6},{8,7},{9,8},{10,9},{11,1... | collective-permute-start | bytes 1572872 | tf_op jit(solution)/shard_map/ppermute | solution.py:25
  52.4 11.7 %copy-start.10 = (bf16[2048,128]{1,0:T(8,128)(2,1)}, bf16[2048,128]{1,0:T(8,128)(2,1)S(1)}, u32[]{:S(2)}) copy-start(bf16[2048,128]{1,0:T(8,128)(2,1)S(1)} %collective-permute-done.2) | copy-start | bytes 1572868
  52.4 11.7 %collective-permute-start.3 = (bf16[2048,128]{1,0:T(8,128)(2,1)S(1)}, bf16[2048,128]{1,0:T(8,128)(2,1)S(1)}, u32[]{:S(2)}, u32[]{:S(2)}) collective-permute-start(bf16[2048,128]{1,0:T(8,128)(2,1)S(1)} %collective-permute-done.2), channel_id=1, source_target_pairs={{0,1},{1,2},{2,3},{3,4},{4,5},{5,6},{6,7},{7,8},{8,9},{9,10},{10,1... | collective-permute-start | bytes 1572872 | tf_op jit(solution)/shard_map/ppermute | solution.py:23
  52.4 5.3 %copy-start.8 = (bf16[2048,128]{1,0:T(8,128)(2,1)}, bf16[2048,128]{1,0:T(8,128)(2,1)S(1)}, u32[]{:S(2)}) copy-start(bf16[2048,128]{1,0:T(8,128)(2,1)S(1)} %collective-permute-done.9) | copy-start | bytes 1572868
  52.5 11.7 %collective-permute-start.10 = (bf16[2048,128]{1,0:T(8,128)(2,1)S(1)}, bf16[2048,128]{1,0:T(8,128)(2,1)S(1)}, u32[]{:S(2)}, u32[]{:S(2)}) collective-permute-start(bf16[2048,128]{1,0:T(8,128)(2,1)S(1)} %collective-permute-done.9), channel_id=1, source_target_pairs={{1,0},{2,1},{3,2},{4,3},{5,4},{6,5},{7,6},{8,7},{9,8},{10,9},{11,1... | collective-permute-start | bytes 1572872 | tf_op jit(solution)/shard_map/ppermute | solution.py:25
  64.1 23.6 %copy-start.15 = (bf16[2048,128]{1,0:T(8,128)(2,1)}, bf16[2048,128]{1,0:T(8,128)(2,1)S(1)}, u32[]{:S(2)}) copy-start(bf16[2048,128]{1,0:T(8,128)(2,1)S(1)} %collective-permute-done.3) | copy-start | bytes 1572868
  64.1 11.4 %collective-permute-start.4 = (bf16[2048,128]{1,0:T(8,128)(2,1)S(1)}, bf16[2048,128]{1,0:T(8,128)(2,1)S(1)}, u32[]{:S(2)}, u32[]{:S(2)}) collective-permute-start(bf16[2048,128]{1,0:T(8,128)(2,1)S(1)} %collective-permute-done.3), channel_id=1, source_target_pairs={{0,1},{1,2},{2,3},{3,4},{4,5},{5,6},{6,7},{7,8},{8,9},{9,10},{10,1... | collective-permute-start | bytes 1572872 | tf_op jit(solution)/shard_map/ppermute | solution.py:23
  64.2 4.9 %copy-start.11 = (bf16[2048,128]{1,0:T(8,128)(2,1)}, bf16[2048,128]{1,0:T(8,128)(2,1)S(1)}, u32[]{:S(2)}) copy-start(bf16[2048,128]{1,0:T(8,128)(2,1)S(1)} %collective-permute-done.10) | copy-start | bytes 1572868
  64.2 11.3 %collective-permute-start.11 = (bf16[2048,128]{1,0:T(8,128)(2,1)S(1)}, bf16[2048,128]{1,0:T(8,128)(2,1)S(1)}, u32[]{:S(2)}, u32[]{:S(2)}) collective-permute-start(bf16[2048,128]{1,0:T(8,128)(2,1)S(1)} %collective-permute-done.10), channel_id=1, source_target_pairs={{1,0},{2,1},{3,2},{4,3},{5,4},{6,5},{7,6},{8,7},{9,8},{10,9},{11,1... | collective-permute-start | bytes 1572872 | tf_op jit(solution)/shard_map/ppermute | solution.py:25
  75.5 17.6 %copy-start.16 = (bf16[2048,128]{1,0:T(8,128)(2,1)}, bf16[2048,128]{1,0:T(8,128)(2,1)S(1)}, u32[]{:S(2)}) copy-start(bf16[2048,128]{1,0:T(8,128)(2,1)S(1)} %collective-permute-done.4) | copy-start | bytes 1572868
  75.5 12.0 %collective-permute-start.5 = (bf16[2048,128]{1,0:T(8,128)(2,1)S(1)}, bf16[2048,128]{1,0:T(8,128)(2,1)S(1)}, u32[]{:S(2)}, u32[]{:S(2)}) collective-permute-start(bf16[2048,128]{1,0:T(8,128)(2,1)S(1)} %collective-permute-done.4), channel_id=1, source_target_pairs={{0,1},{1,2},{2,3},{3,4},{4,5},{5,6},{6,7},{7,8},{8,9},{9,10},{10,1... | collective-permute-start | bytes 1572872 | tf_op jit(solution)/shard_map/ppermute | solution.py:23
  75.5 0.8 copy-start.13
  76.3 11.4 %collective-permute-start.12 = (bf16[2048,128]{1,0:T(8,128)(2,1)S(1)}, bf16[2048,128]{1,0:T(8,128)(2,1)}, u32[]{:S(2)}, u32[]{:S(2)}) collective-permute-start(bf16[2048,128]{1,0:T(8,128)(2,1)S(1)} %collective-permute-done.11), channel_id=1, source_target_pairs={{1,0},{2,1},{3,2},{4,3},{5,4},{6,5},{7,6},{8,7},{9,8},{10,9},{11,1... | collective-permute-start | bytes 1572872 | tf_op jit(solution)/shard_map/ppermute | solution.py:25
  87.5 13.2 %copy-start.17 = (bf16[2048,128]{1,0:T(8,128)(2,1)}, bf16[2048,128]{1,0:T(8,128)(2,1)S(1)}, u32[]{:S(2)}) copy-start(bf16[2048,128]{1,0:T(8,128)(2,1)S(1)} %collective-permute-done.5) | copy-start | bytes 1572868
  87.5 13.2 %collective-permute-start.6 = (bf16[2048,128]{1,0:T(8,128)(2,1)S(1)}, bf16[2048,128]{1,0:T(8,128)(2,1)}, u32[]{:S(2)}, u32[]{:S(2)}) collective-permute-start(bf16[2048,128]{1,0:T(8,128)(2,1)S(1)} %collective-permute-done.5), channel_id=1, source_target_pairs={{0,1},{1,2},{2,3},{3,4},{4,5},{5,6},{6,7},{7,8},{8,9},{9,10},{10,1... | collective-permute-start | bytes 1572872 | tf_op jit(solution)/shard_map/ppermute | solution.py:23
  87.7 15.0 %collective-permute-start.13 = (bf16[2048,128]{1,0:T(8,128)(2,1)}, bf16[2048,128]{1,0:T(8,128)(2,1)}, u32[]{:S(2)}, u32[]{:S(2)}) collective-permute-start(bf16[2048,128]{1,0:T(8,128)(2,1)} %collective-permute-done.12), channel_id=1, source_target_pairs={{1,0},{2,1},{3,2},{4,3},{5,4},{6,5},{7,6},{8,7},{9,8},{10,9},{11,1... | collective-permute-start | bytes 1572872 | tf_op jit(solution)/shard_map/ppermute | solution.py:25
  100.7 14.2 %collective-permute-start.7 = (bf16[2048,128]{1,0:T(8,128)(2,1)}, bf16[2048,128]{1,0:T(8,128)(2,1)}, u32[]{:S(2)}, u32[]{:S(2)}) collective-permute-start(bf16[2048,128]{1,0:T(8,128)(2,1)} %collective-permute-done.6), channel_id=1, source_target_pairs={{0,1},{1,2},{2,3},{3,4},{4,5},{5,6},{6,7},{7,8},{8,9},{9,10},{10,1... | collective-permute-start | bytes 1572872 | tf_op jit(solution)/shard_map/ppermute | solution.py:23
  102.0 28.1 %copy-start.6 = (bf16[2048,128]{1,0:T(8,128)(2,1)S(1)}, bf16[2048,128]{1,0:T(8,128)(2,1)}, u32[]{:S(2)}) copy-start(bf16[2048,128]{1,0:T(8,128)(2,1)} %copy-done.5) | copy-start | bytes 1572868
  102.0 28.9 %copy-start.9 = (bf16[2048,128]{1,0:T(8,128)(2,1)S(1)}, bf16[2048,128]{1,0:T(8,128)(2,1)}, u32[]{:S(2)}) copy-start(bf16[2048,128]{1,0:T(8,128)(2,1)} %copy-done.8) | copy-start | bytes 1572868
  102.0 29.7 %copy-start.12 = (bf16[2048,128]{1,0:T(8,128)(2,1)S(1)}, bf16[2048,128]{1,0:T(8,128)(2,1)}, u32[]{:S(2)}) copy-start(bf16[2048,128]{1,0:T(8,128)(2,1)} %copy-done.11) | copy-start | bytes 1572868
  102.0 30.6 %copy-start.14 = (bf16[2048,128]{1,0:T(8,128)(2,1)S(1)}, bf16[2048,128]{1,0:T(8,128)(2,1)}, u32[]{:S(2)}) copy-start(bf16[2048,128]{1,0:T(8,128)(2,1)} %copy-done.13) | copy-start | bytes 1572868
  102.7 34.4 %collective-permute-start.14 = (bf16[2048,128]{1,0:T(8,128)(2,1)}, bf16[2048,128]{1,0:T(8,128)(2,1)S(1)}, u32[]{:S(2)}, u32[]{:S(2)}) collective-permute-start(bf16[2048,128]{1,0:T(8,128)(2,1)} %collective-permute-done.13), channel_id=1, source_target_pairs={{1,0},{2,1},{3,2},{4,3},{5,4},{6,5},{7,6},{8,7},{9,8},{10,9},{11,1... | collective-permute-start | bytes 1572872 | tf_op jit(solution)/shard_map/ppermute | solution.py:25
  206.3 79.3 %copy-start.3 = (f32[4,512,128]{2,1,0:T(8,128)S(1)}, f32[4,512,128]{2,1,0:T(8,128)}, u32[]{:S(2)}) copy-start(f32[4,512,128]{2,1,0:T(8,128)} %param.14) | copy-start | bytes 3145732
  206.3 79.3 %copy-start.4 = (f32[4,512,128]{2,1,0:T(8,128)S(1)}, f32[4,512,128]{2,1,0:T(8,128)}, u32[]{:S(2)}) copy-start(f32[4,512,128]{2,1,0:T(8,128)} %param.15) | copy-start | bytes 3145732
  206.3 81.0 %copy-start.18 = (s32[16,1]{0,1:T(1,128)S(1)}, s32[16,1]{0,1:T(1,128)}, u32[]{:S(2)}) copy-start(s32[16,1]{0,1:T(1,128)} %param.12) | copy-start | bytes 196
  206.3 149.5 %all-gather.2.cloned.1.call-start = ((), (), s32[]{:S(2)}) async-start(), calls=%async_computation.1 | async-start | bytes 8912896 | tf_op jit(solution)/shard_map/all_gather | solution.py:63
  289.8 69.1 %copy-start.1 = (bf16[2048,512]{1,0:T(8,128)(2,1)S(1)}, bf16[2048,512]{1,0:T(8,128)(2,1)}, u32[]{:S(2)}) copy-start(bf16[2048,512]{1,0:T(8,128)(2,1)} %param.9) | copy-start | bytes 6291460
Sparse Core Ops, SparseCore 0:
  206.4 77.2 reduce-scatter.3
  287.4 68.2 all-gather.1
